TPU v7x, 256 devices: a whole 4x4x8 slice. The times are simulated.
256 devices in a mesh: row: 16 (over x, y), col: 16 (over z, core).
Axes of the slice: x: 4, y: 4, z: 8, core: 2. Of those that a mesh axis runs over, the one named last changes fastest.
Arguments:
- g_hist: bfloat16 [160, 160, 2, 128, 128], P('row', 'col'), may hold values from -6 to 6
- hamiltonian: float32 [2, 128, 128], replicated, may hold values from -0.5 to 0.5
- interaction: float32 [128], replicated, may hold values from 0.1 to 0.4
- partner: int32 [128], replicated, may hold values from 0 to 127, as said below
- order: int32 [160], replicated, may hold values from 0 to 159, each once
Outputs:
- new_row: float32 [160, 2, 128, 128], P('row', None, 'col')
Inputs may be any that keep to these rules, and one draw needn't show every extreme that they name: partner[partner[a]] = a and partner[a] != a for every orbital a.
All inputs are finite; a program needn't handle non-finite values.
Results may differ from a plain program's by a relative error of at most 0.0025.
Values may be sent and summed in bfloat16 or wider, within the bound.
A program may use at most 64 MiB of HBM per device.

v0:
```python
import jax
import jax.numpy as jnp
from jax import lax
from jax.sharding import PartitionSpec as P

time_step = 0.1


def broadcast(shard, axis, root):
    mine = lax.axis_index(axis) == root
    return lax.psum(jnp.where(mine, shard, jnp.zeros_like(shard)), axis)


def sigma_of(rows, interaction, select):
    real = rows[:, 0].astype(jnp.float32)
    imag = rows[:, 1].astype(jnp.float32)
    magnitude = real * real + imag * imag
    swapped = jnp.einsum(
        "ac,kcd,bd->kab", select, magnitude, select, precision=lax.Precision.HIGHEST
    )
    factor = -(interaction[:, None] * interaction[None, :])[None] * swapped
    return jnp.stack([factor * real, factor * imag], 1).astype(jnp.bfloat16)


def stack_terms(sig):
    real = sig[:, 0]
    imag = sig[:, 1]
    first = jnp.stack([-real, -imag], 1)
    second = jnp.stack([-imag, real], 1)
    return jnp.transpose(jnp.stack([first, second], 0), (3, 0, 1, 2, 4))


def contract(stacked, masked):
    out = lax.dot_general(
        stacked, masked, (((2, 3, 4), (1, 2, 4)), ((), ())), preferred_element_type=jnp.float32
    )
    return time_step * out


def apply_matrix(hamiltonian, field):
    high = lax.Precision.HIGHEST
    real = jnp.einsum("ac,kcb->kab", hamiltonian[0], field[:, 0], precision=high) - jnp.einsum(
        "ac,kcb->kab", hamiltonian[1], field[:, 1], precision=high
    )
    imag = jnp.einsum("ac,kcb->kab", hamiltonian[0], field[:, 1], precision=high) + jnp.einsum(
        "ac,kcb->kab", hamiltonian[1], field[:, 0], precision=high
    )
    return jnp.stack([real, imag], 1)


def predict(base, applied, memory):
    return jnp.stack(
        [
            base[:, 0] + time_step * applied[:, 1] + memory[:, 1],
            base[:, 1] - time_step * applied[:, 0] - memory[:, 0],
        ],
        1,
    ).astype(jnp.bfloat16)


def shards(g_hist, hamiltonian, interaction, partner, order):
    row_blocks = g_hist.shape[0]
    col_blocks = g_hist.shape[1]
    orbitals = g_hist.shape[3]
    row_count = lax.axis_size("row")
    col_count = lax.axis_size("col")
    row_index = lax.axis_index("row")
    col_index = lax.axis_index("col")
    slice_rows = orbitals // col_count
    total = order.shape[0]
    positions = jnp.arange(total, dtype=jnp.int32)
    latest = jnp.sum(jnp.where(order == total - 1, positions, 0))
    owner_col = latest // col_blocks
    within = latest - owner_col * col_blocks
    row_times = lax.dynamic_slice_in_dim(order, row_index * row_blocks, row_blocks)
    col_times = lax.dynamic_slice_in_dim(order, col_index * col_blocks, col_blocks)
    valid = col_times[None, :] >= row_times[:, None]
    masked = jnp.where(valid[:, :, None, None, None], g_hist, jnp.zeros((), g_hist.dtype))
    select = (partner[:, None] == jnp.arange(orbitals, dtype=jnp.int32)[None, :]).astype(
        jnp.float32
    )
    column = lax.dynamic_index_in_dim(g_hist, within, 1, keepdims=False)
    column = broadcast(column, "col", owner_col)
    previous = jnp.stack([-jnp.swapaxes(column[:, 0], 1, 2), jnp.swapaxes(column[:, 1], 1, 2)], 1)
    source_row = col_index * row_count // col_count
    sigma_prev = sigma_of(previous, interaction, select)
    shared_prev = broadcast(sigma_prev, "row", source_row)
    stacked_prev = stack_terms(shared_prev)
    a_start = col_index * slice_rows
    ham_rows = lax.dynamic_slice_in_dim(hamiltonian, a_start, slice_rows, 1)
    prev_f = previous.astype(jnp.float32)
    prev_slice = lax.dynamic_slice_in_dim(prev_f, a_start, slice_rows, 2)
    share = lax.psum_scatter(contract(stacked_prev, masked), "col", scatter_dimension=0, tiled=True)
    memory_prev = jnp.transpose(share, (2, 1, 0, 3))
    applied_prev = apply_matrix(ham_rows, prev_f)
    mine = predict(prev_slice, applied_prev, memory_prev)
    predicted = lax.all_gather(mine, "col", axis=2, tiled=True)
    sigma_new = sigma_of(predicted, interaction, select)
    shared_new = broadcast(sigma_new, "row", source_row)
    stacked_new = stack_terms(shared_new)
    memory_new = jnp.transpose(
        lax.psum_scatter(contract(stacked_new, masked), "col", scatter_dimension=0, tiled=True),
        (2, 1, 0, 3),
    )
    applied_new = apply_matrix(ham_rows, predicted.astype(jnp.float32))
    real = prev_slice[:, 0] + 0.5 * (
        time_step * (applied_prev[:, 1] + applied_new[:, 1]) + memory_prev[:, 1] + memory_new[:, 1]
    )
    imag = prev_slice[:, 1] - 0.5 * (
        time_step * (applied_prev[:, 0] + applied_new[:, 0]) + memory_prev[:, 0] + memory_new[:, 0]
    )
    return jnp.stack([real, imag], 1)


def solution(mesh):
    in_specs = (P("row", "col", None, None, None), P(), P(), P(), P())
    out_specs = P("row", None, "col", None)
    return jax.shard_map(shards, mesh=mesh, in_specs=in_specs, out_specs=out_specs, check_vma=False)
```

profile of v0, /device:TPU:1, one launch (start us, length us, event | category | flops | bytes accessed | tf_op | source)
XLA Modules:
  0.0 475.7 jit_solution(16076025068372917322)
XLA Ops:
  6.5 1.4 fusion.89
  10.5 1.1 constant_dynamic-slice_fusion
  11.7 0.3 copy.18
  12.0 0.9 select_bitcast_fusion
  13.1 114.0 %all-reduce.4.cloned.1.call-done = bf16[10,2,128,128]{2,3,0,1:T(8,128)(2,1)} async-done(((bf16[10,2,128,128]{2,3,0,1:T(8,128)(2,1)}), bf16[10,2,128,128]{2,3,0,1:T(8,128)(2,1)}) %all-reduce.4.cloned.1.call-update) | async-done | bytes 655376 | tf_op jit(solution)/shard_map/psum | solution.py:11
  127.1 1.8 fusion.37
  128.9 0.6 fusion.49
  129.5 0.9 maximum_select_fusion
  130.7 94.4 %all-reduce.6.cloned.1.call-done = bf16[10,2,128,128]{3,2,0,1:T(8,128)(2,1)} async-done(((bf16[10,2,128,128]{3,2,0,1:T(8,128)(2,1)}), bf16[10,2,128,128]{3,2,0,1:T(8,128)(2,1)}) %all-reduce.6.cloned.1.call-update) | async-done | bytes 655376 | tf_op jit(solution)/shard_map/psum | solution.py:11
  225.1 1.2 slice_negate_fusion.7
  226.3 0.1 maximum_bitcast_fusion.2
  226.4 5.9 %fusion.9 = f32[128,2,10,128]{3,0,2,1:T(8,128)} fusion(bf16[10,10,2,128,128]{4,3,2,1,0:T(8,128)(2,1)} %param.5, pred[10,10]{1,0:T(8,128)(4,1)S(1)} %broadcast_compare_fusion, bf16[1,10,2,128,128]{4,3,1,2,0:T(8,128)(2,1)S(1)} %get-tuple-element.20, bf16[1,10,2,128,128]{4,3,1,2,0:T(8,128)(2,1)S(1)} %get-tuple-element.19), kind=kOutput, calls=%fused_computation.8 | convolution fusion | flops 1681981440 | bytes 9175140 | tf_op jit(solution)/shard_map/dot_general | solution.py:34
  232.5 0.2 fusion.55
  232.8 0.3 fusion.52
  233.0 0.3 convolution_add_fusion.1
  233.3 0.3 convolution_subtract_fusion.1
  233.5 54.6 %reduce-scatter.3.cloned.1.call-done = f32[8,2,10,128]{3,0,2,1:T(8,128)} async-done(((f32[128,2,10,128]{3,0,2,1:T(8,128)}), f32[8,2,10,128]{3,0,2,1:T(8,128)}) %reduce-scatter.3.cloned.1.call-update) | async-done | bytes 81936 | tf_op jit(solution)/shard_map/reduce_scatter | solution.py:93
  288.2 0.8 fusion.78
  289.0 19.6 %all_gather.3 = bf16[10,2,128,128]{3,2,0,1:T(8,128)(2,1)S(1)} all-gather(bf16[10,2,8,128]{3,2,0,1:T(8,128)(2,1)S(1)} %pad_maximum_fusion.1), channel_id=1, replica_groups=mesh['row'=16,'col'=16] {'col'}, dimensions={2}, use_global_device_ids=true | all-gather | bytes 696320 | tf_op jit(solution)/shard_map/all_gather | solution.py:97
  308.6 0.6 fusion.42
  309.2 0.6 fusion.47
  309.8 0.9 maximum_select_fusion.1
  310.8 92.5 %all-reduce.8.cloned.1.call-done = bf16[10,2,128,128]{3,2,0,1:T(8,128)(2,1)} async-done(((bf16[10,2,128,128]{3,2,0,1:T(8,128)(2,1)}), bf16[10,2,128,128]{3,2,0,1:T(8,128)(2,1)}) %all-reduce.8.cloned.1.call-update) | async-done | bytes 655376 | tf_op jit(solution)/shard_map/psum | solution.py:11
  403.3 1.2 slice_negate_fusion.6
  404.5 0.1 maximum_bitcast_fusion.4
  404.6 5.9 %fusion.15 = f32[128,2,10,128]{3,0,2,1:T(8,128)} fusion(bf16[10,10,2,128,128]{4,3,2,1,0:T(8,128)(2,1)} %param.5, pred[10,10]{1,0:T(8,128)(4,1)S(1)} %broadcast_compare_fusion, bf16[1,10,2,128,128]{4,3,1,2,0:T(8,128)(2,1)S(1)} %get-tuple-element.18, bf16[1,10,2,128,128]{4,3,1,2,0:T(8,128)(2,1)S(1)} %get-tuple-element.17), kind=kOutput, calls=%fused_computation.10 | convolution fusion | flops 1681981440 | bytes 9175140 | tf_op jit(solution)/shard_map/dot_general | solution.py:34
  410.6 0.2 fusion.58
  410.8 0.3 fusion.59
  411.1 55.3 %reduce-scatter.5.cloned.1.call-done = f32[8,2,10,128]{3,0,2,1:T(8,128)} async-done(((f32[128,2,10,128]{3,0,2,1:T(8,128)}), f32[8,2,10,128]{3,0,2,1:T(8,128)}) %reduce-scatter.5.cloned.1.call-update) | async-done | bytes 81936 | tf_op jit(solution)/shard_map/reduce_scatter | solution.py:102
  466.4 1.0 fusion.35
  467.4 1.0 fusion.27
  468.5 0.6 copy.9
  (29 shorter events, 0.6 us)
Async XLA Ops:
  6.5 226.0 %copy-start = (f32[2,128,128]{2,1,0:T(8,128)S(1)}, f32[2,128,128]{2,1,0:T(8,128)}, u32[]{:S(2)}) copy-start(f32[2,128,128]{2,1,0:T(8,128)} %param.6) | copy-start | bytes 393220
  6.5 120.6 %all-reduce.4.cloned.1.call-start = ((), (), s32[]{:S(2)}) async-start(), calls=%async_computation.2 | async-start | bytes 1310720 | tf_op jit(solution)/shard_map/psum | solution.py:11
  12.0 1.0 copy-start.4
  12.0 115.1 %copy-start.3 = (s32[128]{0:T(128)S(1)}, s32[128]{0:T(128)}, u32[]{:S(2)}) copy-start(s32[128]{0:T(128)} %param.8) | copy-start | bytes 1540
  13.0 212.1 %all-reduce.6.cloned.1.call-start = ((), (), s32[]{:S(2)}) async-start(), calls=%async_computation.3 | async-start | bytes 1310720 | tf_op jit(solution)/shard_map/psum | solution.py:11
  127.1 1.8 copy-start.1
  129.5 1.0 copy-start.5
  130.5 157.7 %reduce-scatter.3.cloned.1.call-start = ((), (), s32[]{:S(2)}) async-start(), calls=%async_computation.4 | async-start | bytes 1392640 | tf_op jit(solution)/shard_map/reduce_scatter | solution.py:93
  232.4 171.0 %all-reduce.8.cloned.1.call-start = ((), (), s32[]{:S(2)}) async-start(), calls=%async_computation.5 | async-start | bytes 1310720 | tf_op jit(solution)/shard_map/psum | solution.py:11
  310.8 155.6 %reduce-scatter.5.cloned.1.call-start = ((), (), s32[]{:S(2)}) async-start(), calls=%async_computation.6 | async-start | bytes 1392640 | tf_op jit(solution)/shard_map/reduce_scatter | solution.py:102
  410.6 55.8 %copy-start.2 = (f32[8,2,10,128]{3,0,2,1:T(8,128)S(1)}, f32[8,2,10,128]{3,0,2,1:T(8,128)}, u32[]{:S(2)}) copy-start(f32[8,2,10,128]{3,0,2,1:T(8,128)} %reduce-scatter.3.cloned.1.call-done) | copy-start | bytes 245764
Sparse Core Ops, SparseCore 0:
  13.1 113.9 all-reduce.3
  130.7 94.3 all-reduce.5
  232.5 55.6 reduce-scatter.2
  310.9 92.3 all-reduce.7
  410.7 55.6 reduce-scatter.4
where the time goes:
time: 478 us; the launch traced here: 476 us
  waiting for transfers between devices  411 us (86%)
  blocking collectives  19.6 us (4%)
  matrix products  18.9 us (4%)
  between operations  16 us (3%)
  other arithmetic  7.8 us (2%)
    psum x3, waiting for transfers between devices, broadcast(): return lax.psum(jnp.where(mine, shard, jnp.zeros_like(shard)), axis)  301 us
    reduce_scatter x1, waiting for transfers between devices, shards(): lax.psum_scatter(contract(stacked_new, masked), 'col', scatter_dimension=...  55.3 us
    reduce_scatter x1, waiting for transfers between devices, shards(): lax.psum_scatter(contract(stacked_prev, masked), 'col', scatter_dimension...  54.6 us
    all_gather x1, blocking collectives, shards(): predicted = lax.all_gather(mine, 'col', axis=2, tiled=True)  19.6 us
    dot_general x2, matrix products, contract(): lax.dot_general(stacked, masked, (((2, 3, 4), (1, 2, 4)), ((), ())), pref...  11.9 us
  transfers between devices with their start and end apart: 5, of which 5 were waited for; matrix products, arithmetic and copies ran while one was open for 0% of the time, Pallas kernels for 0%

commit v1 on v0

v1 whole, which is shorter than its diff:
```python
import functools

import jax
import jax.numpy as jnp
from jax import lax
from jax.experimental import pallas as pl
from jax.experimental.pallas import tpu as pltpu
from jax.sharding import PartitionSpec as P

MESH = pl.DeviceIdType.MESH
time_step = 0.1
O = 128
B = 10
ROWS = B * O
PIECE = ROWS // 16
HALF = ROWS // 2
FAR = (4, 3, 5, 2, 6, 1, 7)


def kernel(
    g_hbm, ham, inter, partner, order, out,
    g, send_a, core_a, z_a, piece_a, got_a, f_prev,
    w, wh, part_b, core_b, comb_b, z_b, piece_b, got_b, f_new,
    send_d, core_d, z_d,
    load_sem, core_ss, core_rs, z_ss, z_rs, t_ss, t_rs, all_ss, all_rs, loc_sem,
):
    r = lax.axis_index("row")
    c = lax.axis_index("col")
    z = c // 2
    k = c % 2
    other = (r, 2 * z + 1 - k)
    bf16 = jnp.bfloat16
    f32 = jnp.float32

    for j in range(B):
        pltpu.make_async_copy(g_hbm.at[j], g.at[j], load_sem.at[j]).start()

    barrier = pltpu.get_barrier_semaphore()
    peers = [other] + [(r, 2 * ((z + d) % 8) + k) for d in range(1, 8)]
    peers += [((r + d) % 16, c) for d in range(1, 16)]
    for peer in peers:
        pl.semaphore_signal(barrier, inc=1, device_id=peer, device_id_type=MESH)

    @pl.when(r != c)
    def _():
        pl.semaphore_signal(barrier, inc=1, device_id=(c, r), device_id_type=MESH)

    def find(i, found):
        for s in range(10):
            found = jnp.where(order[i * 10 + s] == 16 * B - 1, i * 10 + s, found)
        return found

    latest = lax.fori_loop(0, 16, find, jnp.int32(0))
    owner = latest // B
    within = latest - owner * B
    mine = jnp.where(owner == c, jnp.float32(1), jnp.float32(0)).astype(bf16)

    for j in range(B):
        pltpu.make_async_copy(g_hbm.at[j], g.at[j], load_sem.at[j]).wait()

    def column(j, carry):
        block = g[j, within]
        at = pl.ds(pl.multiple_of(j * O, O), O)
        send_a[at, :O] = -block[0] * mine
        send_a[at, O:] = block[1] * mine
        return carry

    lax.fori_loop(0, B, column, 0)

    @pl.when(r != c)
    def _():
        pl.semaphore_wait(barrier, len(peers) + 1)

    @pl.when(r == c)
    def _():
        pl.semaphore_wait(barrier, len(peers))

    def rows(start, size):
        return pl.ds(pl.multiple_of(start, 16), size)

    def remote(src, dst, ss, rs, to):
        return pltpu.make_async_remote_copy(
            src_ref=src, dst_ref=dst, send_sem=ss, recv_sem=rs, device_id=to, device_id_type=MESH
        )

    def z_sends(src_of, dst, phase):
        copies = []
        for d in FAR:
            zz = (z + d) % 8
            copy = remote(src_of(zz), dst.at[d], z_ss.at[phase, d], z_rs.at[phase, d], (r, 2 * zz + k))
            copy.start()
            copies.append(copy)
        return copies

    q = (r % 2) * 8 + r // 2

    def gather(piece, got, f, phase):
        @pl.when(r != c)
        def _():
            copy = remote(piece, got, t_ss.at[phase], t_rs.at[phase], (c, r))
            copy.start()
            copy.wait()

        @pl.when(r == c)
        def _():
            copy = pltpu.make_async_copy(piece, got, loc_sem.at[phase])
            copy.start()
            copy.wait()

        copies = []
        for d in range(1, 16):
            copy = remote(
                got, f.at[rows(q * PIECE, PIECE)], all_ss.at[phase, d], all_rs.at[phase, d], ((r + d) % 16, c)
            )
            copy.start()
            copies.append(copy)
        f[rows(q * PIECE, PIECE)] = got[...]
        return copies

    def gathered(copies):
        for copy in copies:
            copy.wait_recv()
        for copy in copies:
            copy.wait_send()

    a_core = remote(
        send_a.at[rows((1 - k) * HALF, HALF)], core_a, core_ss.at[0], core_rs.at[0], other
    )
    a_core.start()

    lane = lax.broadcasted_iota(jnp.int32, (O, O), 1)
    sub = lax.broadcasted_iota(jnp.int32, (O, O), 0)
    select = jnp.where(partner[...] == sub, jnp.float32(1), jnp.float32(0)).astype(bf16)
    u_row = inter[...]
    u_col = jnp.sum(jnp.where(lane == sub, jnp.broadcast_to(u_row, (O, O)), 0.0), axis=1, keepdims=True)
    strength = -(u_col * u_row)

    a_core.wait_recv()
    own = rows(k * HALF, HALF)
    send_a[own] = send_a[own] + core_a[...]
    a_z = z_sends(lambda zz: send_a.at[rows(k * HALF + zz * PIECE, PIECE)], z_a, 0)

    h_re = ham[0].T
    h_im = ham[1].T
    h_all = jnp.concatenate(
        [jnp.concatenate([h_im, -h_re], axis=1), jnp.concatenate([h_re, h_im], axis=1)], axis=0
    )
    high = h_all.astype(bf16)
    rest = h_all - high.astype(f32)
    mid = rest.astype(bf16)
    wh[0] = high
    wh[1] = mid
    wh[2] = (rest - mid.astype(f32)).astype(bf16)

    def mask(j, carry):
        row_time = order[r * B + j]
        for kk in range(B):
            keep = jnp.where(order[c * B + kk] >= row_time, jnp.float32(1), jnp.float32(0)).astype(bf16)
            g[j, kk] = g[j, kk] * keep
        return carry

    lax.fori_loop(0, B, mask, 0)

    total = send_a[rows(k * HALF + z * PIECE, PIECE)]
    for copy, d in zip(a_z, FAR):
        copy.wait_recv()
        total = total + z_a[d]
    piece_a[...] = total
    a_all = gather(piece_a, got_a, f_prev, 0)
    gathered(a_all)

    def self_energy(f):
        def one(n, carry):
            at = pl.ds(pl.multiple_of(n * O, O), O)
            re = f[at, :O]
            im = f[at, O:]
            both = jnp.concatenate([re, im], axis=0)
            turned = jnp.dot(both, select, preferred_element_type=f32).astype(bf16)
            turned = jnp.concatenate([turned[:O], turned[O:]], axis=1)
            turned = jnp.dot(select, turned, preferred_element_type=f32)
            t_re = turned[:, :O]
            t_im = turned[:, O:]
            factor = strength * (t_re * t_re + t_im * t_im)
            s_re = (factor * re.astype(f32)).astype(bf16)
            s_im = (factor * im.astype(f32)).astype(bf16)
            w[n, :O, :O] = -s_im
            w[n, :O, O:] = s_re
            w[n, O:, :O] = s_re
            w[n, O:, O:] = s_im
            return carry

        lax.fori_loop(0, B, one, 0)

    def contract(j):
        acc = jnp.zeros((O, 2 * O), f32)
        for kk in range(B):
            left = jnp.concatenate([g[j, kk, 0], g[j, kk, 1]], axis=1)
            acc += jnp.dot(left, w[kk], preferred_element_type=f32)
        return acc

    def hamiltonian(f, at):
        left = f[at]
        acc = jnp.dot(left, wh[2], preferred_element_type=f32)
        acc += jnp.dot(left, wh[1], preferred_element_type=f32)
        acc += jnp.dot(left, wh[0], preferred_element_type=f32)
        return acc

    self_energy(f_prev)

    def share_b(n, carry):
        j = ((1 - k) * 5 + n) % B
        at = pl.ds(pl.multiple_of(j * O, O), O)
        part_b[at] = time_step * contract(j)

        @pl.when(r == c)
        def _():
            part_b[at] += time_step * hamiltonian(f_prev, at) + f_prev[at].astype(f32)

        return carry

    lax.fori_loop(0, 5, share_b, 0)
    b_core = remote(
        part_b.at[rows((1 - k) * HALF, HALF)], core_b, core_ss.at[1], core_rs.at[1], other
    )
    b_core.start()
    lax.fori_loop(5, 10, share_b, 0)
    b_core.wait_recv()
    comb_b[...] = part_b[own] + core_b[...]
    b_z = z_sends(lambda zz: comb_b.at[rows(zz * PIECE, PIECE)], z_b, 1)
    total = comb_b[rows(z * PIECE, PIECE)]
    for copy, d in zip(b_z, FAR):
        copy.wait_recv()
        total = total + z_b[d]
    piece_b[...] = total.astype(bf16)
    b_all = gather(piece_b, got_b, f_new, 1)
    gathered(b_all)

    self_energy(f_new)

    def share_d(j, carry):
        at = pl.ds(pl.multiple_of(j * O, O), O)
        part_b[at] = 0.5 * part_b[at] + (0.5 * time_step) * contract(j)

        @pl.when(r == c)
        def _():
            part_b[at] += (0.5 * time_step) * hamiltonian(f_new, at) + 0.5 * f_prev[at].astype(f32)

        for o in range(2):
            turned = part_b[at, o * O:(o + 1) * O].T.reshape(8, 2, 8, O)
            for kk in range(2):
                send_d[kk, :, 2 * j + o] = turned[:, kk]
        return carry

    b_core.wait_send()
    lax.fori_loop(0, B, share_d, 0)
    d_core = remote(send_d.at[1 - k], core_d, core_ss.at[2], core_rs.at[2], other)
    d_core.start()
    d_core.wait()
    send_d[k] = send_d[k] + core_d[...]
    d_z = z_sends(lambda zz: send_d.at[k, zz], z_d, 2)
    total = send_d[k, z]
    for copy, d in zip(d_z, FAR):
        copy.wait_recv()
        total = total + z_d[d]
    out[...] = total.reshape(B, 2, 8, O)

    a_core.wait_send()
    for copies in (a_z, b_z, d_z):
        for copy in copies:
            copy.wait_send()


def shards(g_hist, hamiltonian, interaction, partner, order):
    bf16 = jnp.bfloat16
    f32 = jnp.float32
    vmem = pltpu.VMEM
    dma = pltpu.SemaphoreType.DMA
    spec = pl.BlockSpec(memory_space=pltpu.VMEM)
    return pl.pallas_call(
        kernel,
        out_shape=jax.ShapeDtypeStruct((B, 2, 8, O), f32),
        in_specs=[
            pl.BlockSpec(memory_space=pl.ANY),
            spec,
            spec,
            spec,
            pl.BlockSpec(memory_space=pltpu.SMEM),
        ],
        out_specs=spec,
        scratch_shapes=[
            vmem((B, B, 2, O, O), bf16),
            vmem((ROWS, 2 * O), bf16),
            vmem((HALF, 2 * O), bf16),
            vmem((8, PIECE, 2 * O), bf16),
            vmem((PIECE, 2 * O), bf16),
            vmem((PIECE, 2 * O), bf16),
            vmem((ROWS, 2 * O), bf16),
            vmem((B, 2 * O, 2 * O), bf16),
            vmem((3, 2 * O, 2 * O), bf16),
            vmem((ROWS, 2 * O), f32),
            vmem((HALF, 2 * O), f32),
            vmem((HALF, 2 * O), f32),
            vmem((8, PIECE, 2 * O), f32),
            vmem((PIECE, 2 * O), bf16),
            vmem((PIECE, 2 * O), bf16),
            vmem((ROWS, 2 * O), bf16),
            vmem((2, 8, 2 * B, 8, O), f32),
            vmem((8, 2 * B, 8, O), f32),
            vmem((8, 2 * B, 8, O), f32),
            dma((B,)),
            dma((3,)),
            dma((3,)),
            dma((3, 8)),
            dma((3, 8)),
            dma((2,)),
            dma((2,)),
            dma((2, 16)),
            dma((2, 16)),
            dma((2,)),
        ],
        compiler_params=pltpu.CompilerParams(
            collective_id=0, has_side_effects=True, vmem_limit_bytes=48 * 2**20
        ),
    )(g_hist, hamiltonian, interaction.reshape(1, O), partner.reshape(1, O), order)


def solution(mesh):
    in_specs = (P("row", "col", None, None, None), P(), P(), P(), P())
    out_specs = P("row", None, "col", None)
    return jax.shard_map(shards, mesh=mesh, in_specs=in_specs, out_specs=out_specs, check_vma=False)
```

time: 478 us -> 108 us (0.23)
  waiting for transfers between devices: 411 us -> 0 us
  Pallas kernels: 0 us -> 105 us
  blocking collectives: 19.6 us -> 0 us
  matrix products: 18.9 us -> 0 us
  between operations: 16 us -> 0.01 us
  other arithmetic: 7.8 us -> 0 us
    psum x3 -> x0, waiting for transfers between devices: 301 us -> none  [broadcast(): return lax.psum(jnp.where(mine, shard, jnp.zeros_like(shard)), axis)]
    reduce_scatter x2 -> x0, waiting for transfers between devices: 110 us -> none  [the longest x1 55.3 us: shards(): lax.psum_scatter(contract(stacked_new, masked), 'col', scatter_dimension=...]
    pallas_call x0 -> x1, Pallas kernels: none -> 105 us  [shards(): pl.pallas_call(kernel, out_shape=jax.ShapeDtypeStruct((B, 2, 8, O), f32),...]
    all_gather x1 -> x0, blocking collectives: 19.6 us -> none  [shards(): predicted = lax.all_gather(mine, 'col', axis=2, tiled=True)]
    dot_general x14 -> x0, matrix products: 18.9 us -> none  [the longest x2 11.9 us: contract(): lax.dot_general(stacked, masked, (((2, 3, 4), (1, 2, 4)), ((), ())), pref...]
  transfers between devices with their start and end apart: 5 -> 0, of which waited for: 5 -> 0; matrix products, arithmetic and copies ran while one was open for 0% -> 0% of each run, Pallas kernels for 0% -> 0%
where the time goes in v1:
time: 108 us
  Pallas kernels  105 us (97%)
  local copies, waits for them, and re-layouts  3.53 us (3%)
    pallas_call x1, Pallas kernels, shards(): pl.pallas_call(kernel, out_shape=jax.ShapeDtypeStruct((B, 2, 8, O), f32),...  105 us
    unnamed x9, local copies, waits for them, and re-layouts  3.53 us

profile of v1, /device:TPU:1, one launch (start us, length us, event | category | flops | bytes accessed | tf_op | source)
XLA Modules:
  0.0 108.2 jit_solution(2930501955232117909)
XLA Ops:
  0.0 0.0 copy-start
  0.0 0.9 copy-done
  0.9 0.0 copy-start.1
  0.9 0.7 copy-done.1
  1.6 0.0 copy-start.2
  1.6 0.7 copy-done.2
  2.2 0.0 copy-start.3
  2.2 0.7 copy-done.3
  2.9 104.7 %shard_map.55 = f32[10,2,8,128]{3,2,1,0:T(8,128)S(1)} custom-call(bf16[10,10,2,128,128]{4,3,2,1,0:T(8,128)(2,1)} %g_hbm.1, f32[2,128,128]{2,1,0:T(8,128)S(1)} %copy-done, f32[1,128]{1,0:T(1,128)S(1)} %bitcast.2, s32[1,128]{1,0:T(1,128)S(1)} %bitcast.3, s32[160]{0:T(256)S(1)} %copy-done.1), custom_call_target="tpu_custom_call" | custom-call | tf_op jit(solution)/shard_map/pallas_call | solution.py:279
  107.6 0.6 copy.7
Async XLA Ops:
  0.0 0.9 copy-start
  0.9 0.7 copy-start.1
  1.6 0.7 copy-start.2
  2.2 0.7 copy-start.3

commit v2 on v0

v2 whole, which is shorter than its diff:
```python
import jax
import jax.numpy as jnp
from jax import lax
from jax.experimental import pallas as pl
from jax.experimental.pallas import tpu as pltpu
from jax.sharding import PartitionSpec as P

MESH = pl.DeviceIdType.MESH
time_step = 0.1
O = 128
B = 10
ROWS = B * O
CHUNKS = ((0, 6), (6, 4))
NC = len(CHUNKS)
FAR = (4, 3, 5, 2, 6, 1, 7)
AROUND = sorted(
    ((dx, dy) for dx in range(4) for dy in range(4) if dx or dy),
    key=lambda o: -(min(o[0], 4 - o[0]) + min(o[1], 4 - o[1])),
)
STEP = (
    (2, 2), (1, 2), (2, 1), (2, 3), (2, 0), (1, 1), (3, 3), (0, 1),
    (3, 0), (0, 0), (0, 3), (1, 0), (1, 3), (3, 1), (3, 2), (0, 2),
)
STEP_X = tuple(s[0] for s in STEP)
STEP_Y = tuple(s[1] for s in STEP)
STEP_OF = tuple(STEP.index((i // 4, i % 4)) for i in range(16))


def look_up(table, index):
    value = jnp.int32(table[0])
    for i in range(1, len(table)):
        value = jnp.where(index == i, jnp.int32(table[i]), value)
    return value


def kernel(
    g_hbm, ham_hbm, inter_hbm, partner_hbm, order_hbm, out,
    g, ham, inter, partner, order,
    send_a, core_a, comb_a, z_a, piece_a, f_prev, w, wh, part,
    core_b, comb_b, z_b, sum_b, piece_b, f_new, z_d, sum_d,
    load_sem, small_sem, core_ss, core_rs, a_ss, a_rs, z_ss, z_rs, t_ss, t_rs, all_ss, all_rs, *chunked,
):
    bf16 = jnp.bfloat16
    f32 = jnp.float32
    r = lax.axis_index("row")
    c = lax.axis_index("col")
    x = r // 4
    y = r % 4
    z = c // 2
    k = c % 2
    other = (r, 2 * z + 1 - k)

    loads = [pltpu.make_async_copy(order_hbm, order, small_sem.at[0])]
    loads += [pltpu.make_async_copy(g_hbm.at[j], g.at[j], load_sem.at[j]) for j in range(B)]
    loads += [
        pltpu.make_async_copy(a, b, small_sem.at[i + 1])
        for i, (a, b) in enumerate(((ham_hbm, ham), (inter_hbm, inter), (partner_hbm, partner)))
    ]
    for load in loads:
        load.start()

    n_out = 2 * ((r // 2 - z + 8) % 8) + k
    to = ((x + look_up(STEP_X, n_out)) % 4 * 4 + (y + look_up(STEP_Y, n_out)) % 4, r)
    q_out = k * 8 + z
    n_in = look_up(STEP_OF, (x - c // 4 + 4) % 4 * 4 + (y - c % 4 + 4) % 4)
    z_in = (c // 2 - n_in // 2 + 8) % 8
    source = (c, 2 * z_in + n_in % 2)
    q_in = n_in % 2 * 8 + z_in
    around = [((x + dx) % 4 * 4 + (y + dy) % 4, c) for dx, dy in AROUND]

    barrier = pltpu.get_barrier_semaphore()
    up = (r, 2 * ((z + 1) % 8) + k)
    down = (r, 2 * ((z + 7) % 8) + k)
    peers = [to, source] + [(r, 2 * ((z + d) % 8) + k) for d in FAR] + around + [other]
    for peer in peers:
        pl.semaphore_signal(barrier, inc=1, device_id=peer, device_id_type=MESH)

    def rows(start, size):
        return pl.ds(pl.multiple_of(start, 16), size)

    def remote(src, dst, ss, rs, device):
        copy = pltpu.make_async_remote_copy(
            src_ref=src, dst_ref=dst, send_sem=ss, recv_sem=rs, device_id=device, device_id_type=MESH
        )
        copy.start()
        sent.append(copy)
        return copy

    sent = []
    send_d = chunked[:NC]
    core_d = chunked[NC:2 * NC]
    comb_d = chunked[2 * NC:]

    def half(ch, core):
        first, n = CHUNKS[ch]
        return rows(first * O + core * (n * O // 2), n * O // 2)

    def piece(ch, q):
        first, n = CHUNKS[ch]
        return rows(first * O + q * (n * 8), n * 8)

    def near(ch):
        first, n = CHUNKS[ch]
        return pl.ds(first * 8, n * 8)

    def core_near(ch):
        first, n = CHUNKS[ch]
        return pl.ds(first * 64, n * 64)

    def core_piece(ch, zz):
        first, n = CHUNKS[ch]
        return rows(first * 64 + zz * (n * 8), n * 8)

    def to_other(src, dst, phase, ch):
        return remote(src, dst, core_ss.at[phase, ch], core_rs.at[phase, ch], other)

    def chain(comb, own, slots, sums, box, halve, phase, ch, step):
        for way, (sign, device) in enumerate(((1, up), (7, down))):
            whole = own((z + sign * (4 - step)) % 8)
            if step == 0:
                src = comb.at[halve(whole, way)]
                dst = slots.at[(way, 0) + halve(box, way)]
            else:
                links[phase, ch, way, step - 1].wait_recv()
                sums[(way, step - 1) + box] = comb[whole]
                came = halve(box, way) if step == 1 else box
                there = (way, step - 1) + came
                sums[there] = sums[there] + slots[there]
                src = sums.at[(way, step - 1) + box]
                dst = slots.at[(way, step) + box]
            links[phase, ch, way, step] = remote(
                src, dst, z_ss.at[phase, ch, way, step], z_rs.at[phase, ch, way, step], device
            )

    def chained(comb, own, slots, box, phase, ch):
        total = comb[own(z)]
        for way in range(2):
            links[phase, ch, way, 3].wait_recv()
            total = total + slots[(way, 3) + box]
        return total

    links = {}

    def lane_half(index, way):
        return index + (pl.ds(way * O, O),)

    def turn(src, f, phase, ch):
        return remote(src, f.at[piece(ch, q_out)], t_ss.at[phase, ch], t_rs.at[phase, ch], to)

    def spread(f, phase, ch):
        return [
            remote(
                f.at[piece(ch, q_in)], f.at[piece(ch, q_in)],
                all_ss.at[phase, ch, i], all_rs.at[phase, ch, i], device,
            )
            for i, device in enumerate(around)
        ]

    def received(copies):
        for copy in copies:
            copy.wait_recv()

    loads[0].wait()

    def find(i, found):
        for s in range(B):
            found = jnp.where(order[i * B + s] == 16 * B - 1, i * B + s, found)
        return found

    latest = lax.fori_loop(0, 16, find, jnp.int32(0))
    owner = latest // B
    within = latest - owner * B
    mine = jnp.where(owner == c, jnp.float32(1), jnp.float32(0)).astype(bf16)

    for load in loads[1:]:
        load.wait()

    for j in range(B):
        block = g[j, within]
        send_a[j * O:(j + 1) * O, :O] = -block[0] * mine
        send_a[j * O:(j + 1) * O, O:] = block[1] * mine

    pl.semaphore_wait(barrier, len(peers))

    a_core = [
        to_other(send_a.at[half(ch, 1 - k)], core_a.at[core_near(ch)], 0, ch) for ch in range(NC)
    ]

    a_z = []
    for ch in range(NC):
        a_core[ch].wait_recv()
        comb_a[core_near(ch)] = send_a[half(ch, k)] + core_a[core_near(ch)]
        a_z.append([
            remote(
                comb_a.at[core_piece(ch, (z + d) % 8)], z_a.at[d - 1, near(ch)],
                a_ss.at[ch, d - 1], a_rs.at[ch, d - 1], (r, 2 * ((z + d) % 8) + k),
            )
            for d in FAR
        ])

    lane = lax.broadcasted_iota(jnp.int32, (O, O), 1)
    sub = lax.broadcasted_iota(jnp.int32, (O, O), 0)
    select = jnp.where(partner[...] == sub, jnp.float32(1), jnp.float32(0)).astype(bf16)
    u_row = inter[...]
    u_col = jnp.sum(
        jnp.where(lane == sub, jnp.broadcast_to(u_row, (O, O)), 0.0), axis=1, keepdims=True
    )
    strength = -(u_col * u_row)
    h_re = ham[0].T
    h_im = ham[1].T
    h_all = jnp.concatenate(
        [jnp.concatenate([h_im, -h_re], axis=1), jnp.concatenate([h_re, h_im], axis=1)], axis=0
    )
    high = h_all.astype(bf16)
    rest = h_all - high.astype(f32)
    mid = rest.astype(bf16)
    wh[0] = high
    wh[1] = mid
    wh[2] = (rest - mid.astype(f32)).astype(bf16)

    def mask(j, carry):
        row_time = order[r * B + j]
        for kk in range(B):
            keep = jnp.where(order[c * B + kk] >= row_time, jnp.float32(1), jnp.float32(0)).astype(bf16)
            g[j, kk] = g[j, kk] * keep
        return carry

    lax.fori_loop(0, B, mask, 0)

    def hamiltonian(left):
        acc = jnp.dot(left, wh[2], preferred_element_type=f32)
        acc += jnp.dot(left, wh[1], preferred_element_type=f32)
        acc += jnp.dot(left, wh[0], preferred_element_type=f32)
        return acc

    def flow(finish, f, phase):
        turns = []
        spreads = []
        for ch in range(NC):
            finish(ch)
            turns.append(turn((piece_a, piece_b)[phase].at[near(ch)], f, phase, ch))
            if ch > 0:
                turns[ch - 1].wait_recv()
                spreads.append(spread(f, phase, ch - 1))
        turns[NC - 1].wait_recv()
        spreads.append(spread(f, phase, NC - 1))
        return spreads

    def finish_a(ch):
        total = comb_a[core_piece(ch, z)]
        for copy, d in zip(a_z[ch], FAR):
            copy.wait_recv()
            total = total + z_a[d - 1, near(ch)]
        piece_a[near(ch)] = total

    a_all = flow(finish_a, f_prev, 0)

    def self_energy(f, ch):
        first, count = CHUNKS[ch]
        for n in range(first, first + count):
            re = f[n * O:(n + 1) * O, :O]
            im = f[n * O:(n + 1) * O, O:]
            both = jnp.concatenate([re, im], axis=0)
            turned = jnp.dot(both, select, preferred_element_type=f32).astype(bf16)
            turned = jnp.concatenate([turned[:O], turned[O:]], axis=1)
            turned = jnp.dot(select, turned, preferred_element_type=f32)
            t_re = turned[:, :O]
            t_im = turned[:, O:]
            factor = strength * (t_re * t_re + t_im * t_im)
            s_re = (factor * re.astype(f32)).astype(bf16)
            s_im = (factor * im.astype(f32)).astype(bf16)
            w[n, :O, :O] = -s_im
            w[n, :O, O:] = s_re
            w[n, O:, :O] = s_re
            w[n, O:, O:] = s_im

    def contract(first, count, ch, fresh):
        at = rows(first * O, count * O)
        start, number = CHUNKS[ch]
        for kk in range(start, start + number):
            left = jnp.concatenate(
                [g[pl.ds(first, count), kk, i].reshape(count * O, O) for i in range(2)], axis=1
            )
            term = jnp.dot(left, w[kk], preferred_element_type=f32)
            if fresh and kk == start:
                part[at] = term
            else:
                part[at] += term

    for ch in range(NC):
        received(a_all[ch])
        self_energy(f_prev, ch)
        if ch < NC - 1:
            contract(0, B, ch, ch == 0)
    b_core = []

    def chain_b(ch, step):
        chain(
            comb_b, lambda zz: (core_piece(ch, zz),), z_b, sum_b, (near(ch),), lane_half, 1, ch, step
        )

    for ch in range(NC):
        first, n = CHUNKS[ch]
        contract(first + (1 - k) * (n // 2), n // 2, NC - 1, False)
        b_core.append(to_other(part.at[half(ch, 1 - k)], core_b.at[core_near(ch)], 1, ch))
        contract(first + k * (n // 2), n // 2, NC - 1, False)
        b_core[ch].wait_recv()
        comb_b[core_near(ch)] = part[half(ch, k)] + core_b[core_near(ch)]
        chain_b(ch, 0)
    for step in range(1, 4):
        for ch in range(NC):
            chain_b(ch, step)
    for copy in b_core:
        copy.wait_send()
    sent[:] = [copy for copy in sent if not any(copy is done for done in b_core)]

    def finish_b(ch):
        first, n = CHUNKS[ch]
        base = piece_a[near(ch)]
        shift = hamiltonian(base)
        total = chained(comb_b, lambda zz: (core_piece(ch, zz),), z_b, (near(ch),), 1, ch)
        base = base.astype(f32)
        new = (base + time_step * (shift + total)).astype(bf16)
        piece_b[near(ch)] = new
        part[piece(ch, q_out)] += (2 / time_step) * base + shift + hamiltonian(new)

    b_all = flow(finish_b, f_new, 1)

    for ch in range(NC):
        received(b_all[ch])
        self_energy(f_new, ch)
        if ch < NC - 1:
            contract(0, B, ch, False)
    d_core = []

    def box_d(ch):
        first, n = CHUNKS[ch]
        return (pl.ds(first * 16, n * 16),)

    def chain_d(ch, step):
        first, n = CHUNKS[ch]

        def row_half(index, way):
            start = first * 16 if len(index) == 1 else 0
            return index[:-1] + (pl.ds(start + way * n * 8, n * 8),)

        chain(
            comb_d[ch], lambda zz: (zz, pl.ds(0, n * 16)), z_d, sum_d, box_d(ch), row_half, 2, ch, step
        )

    def over_z_d(ch):
        first, n = CHUNKS[ch]
        d_core[ch].wait_recv()
        comb_d[ch][...] = send_d[ch][k] + core_d[ch][...]
        chain_d(ch, 0)

    for ch in range(NC):
        first, n = CHUNKS[ch]
        contract(first, n, NC - 1, False)
        for j in range(first, first + n):
            for o in range(2):
                turned = part[j * O:(j + 1) * O, o * O:(o + 1) * O].T.reshape(8, 2, 8, O)
                at = pl.ds((2 * (j - first) + o) * 8, 8)
                for kk in range(2):
                    send_d[ch][kk, :, at] = turned[:, kk]
        d_core.append(to_other(send_d[ch].at[1 - k], core_d[ch], 2, ch))
        if ch > 0:
            over_z_d(ch - 1)
    over_z_d(NC - 1)
    for step in range(1, 4):
        for ch in range(NC):
            chain_d(ch, step)
    for ch in range(NC):
        first, n = CHUNKS[ch]
        total = chained(comb_d[ch], lambda zz: (zz, pl.ds(0, n * 16)), z_d, box_d(ch), 2, ch)
        out[first:first + n] = (0.5 * time_step) * total.reshape(n, 2, 8, O)

    for copy in sent:
        copy.wait_send()


def shards(g_hist, hamiltonian, interaction, partner, order):
    bf16 = jnp.bfloat16
    f32 = jnp.float32
    vmem = pltpu.VMEM
    dma = pltpu.SemaphoreType.DMA
    return pl.pallas_call(
        kernel,
        out_shape=jax.ShapeDtypeStruct((B, 2, 8, O), f32),
        in_specs=[pl.BlockSpec(memory_space=pltpu.HBM)] * 5,
        out_specs=pl.BlockSpec(memory_space=pltpu.VMEM),
        scratch_shapes=[
            vmem((B, B, 2, O, O), bf16),
            vmem((2, O, O), f32),
            vmem((1, O), f32),
            vmem((1, O), jnp.int32),
            pltpu.SMEM((16 * B,), jnp.int32),
            vmem((ROWS, 2 * O), bf16),
            vmem((ROWS // 2, 2 * O), bf16),
            vmem((ROWS // 2, 2 * O), bf16),
            vmem((7, ROWS // 16, 2 * O), bf16),
            vmem((ROWS // 16, 2 * O), bf16),
            vmem((ROWS, 2 * O), bf16),
            vmem((B, 2 * O, 2 * O), bf16),
            vmem((3, 2 * O, 2 * O), bf16),
            vmem((ROWS, 2 * O), f32),
            vmem((ROWS // 2, 2 * O), f32),
            vmem((ROWS // 2, 2 * O), f32),
            vmem((2, 4, ROWS // 16, 2 * O), f32),
            vmem((2, 3, ROWS // 16, 2 * O), f32),
            vmem((ROWS // 16, 2 * O), bf16),
            vmem((ROWS, 2 * O), bf16),
            vmem((2, 4, 16 * B, O), f32),
            vmem((2, 3, 16 * B, O), f32),
            dma((B,)),
            dma((4,)),
            dma((3, NC)),
            dma((3, NC)),
            dma((NC, 7)),
            dma((NC, 7)),
            dma((3, NC, 2, 4)),
            dma((3, NC, 2, 4)),
            dma((2, NC)),
            dma((2, NC)),
            dma((2, NC, 15)),
            dma((2, NC, 15)),
        ]
        + [vmem((2, 8, 16 * n, O), f32) for _, n in CHUNKS]
        + [vmem((8, 16 * n, O), f32) for _, n in CHUNKS] * 2,
        compiler_params=pltpu.CompilerParams(
            collective_id=0, has_side_effects=True, vmem_limit_bytes=60 * 2**20
        ),
    )(g_hist, hamiltonian, interaction.reshape(1, O), partner.reshape(1, O), order)


def solution(mesh):
    in_specs = (P("row", "col", None, None, None), P(), P(), P(), P())
    out_specs = P("row", None, "col", None)
    return jax.shard_map(shards, mesh=mesh, in_specs=in_specs, out_specs=out_specs, check_vma=False)
```

time: 478 us -> 85.6 us (0.18)
  waiting for transfers between devices: 411 us -> 0 us
  Pallas kernels: 0 us -> 84 us
  blocking collectives: 19.6 us -> 0 us
  matrix products: 18.9 us -> 0 us
  between operations: 16 us -> 0.01 us
  other arithmetic: 7.8 us -> 0 us
    psum x3 -> x0, waiting for transfers between devices: 301 us -> none  [broadcast(): return lax.psum(jnp.where(mine, shard, jnp.zeros_like(shard)), axis)]
    reduce_scatter x2 -> x0, waiting for transfers between devices: 110 us -> none  [the longest x1 55.3 us: shards(): lax.psum_scatter(contract(stacked_new, masked), 'col', scatter_dimension=...]
    pallas_call x0 -> x1, Pallas kernels: none -> 84 us  [shards(): pl.pallas_call(kernel, out_shape=jax.ShapeDtypeStruct((B, 2, 8, O), f32),...]
    all_gather x1 -> x0, blocking collectives: 19.6 us -> none  [shards(): predicted = lax.all_gather(mine, 'col', axis=2, tiled=True)]
    dot_general x14 -> x0, matrix products: 18.9 us -> none  [the longest x2 11.9 us: contract(): lax.dot_general(stacked, masked, (((2, 3, 4), (1, 2, 4)), ((), ())), pref...]
  transfers between devices with their start and end apart: 5 -> 0, of which waited for: 5 -> 0; matrix products, arithmetic and copies ran while one was open for 0% -> 0% of each run, Pallas kernels for 0% -> 0%
where the time goes in v2:
time: 85.6 us; the launch traced here: 85.5 us
  Pallas kernels  84 us (98%)
  local copies, waits for them, and re-layouts  1.53 us (2%)
    pallas_call x1, Pallas kernels, shards(): pl.pallas_call(kernel, out_shape=jax.ShapeDtypeStruct((B, 2, 8, O), f32),...  84 us

profile of v2, /device:TPU:1, one launch (start us, length us, event | category | flops | bytes accessed | tf_op | source)
XLA Modules:
  0.0 85.5 jit_solution(11618583968946816040)
XLA Ops:
  0.0 84.0 %shard_map.55 = f32[10,2,8,128]{3,2,1,0:T(8,128)} custom-call(bf16[10,10,2,128,128]{4,3,2,1,0:T(8,128)(2,1)} %g_hbm.1, f32[2,128,128]{2,1,0:T(8,128)} %ham_hbm.1, f32[1,128]{1,0:T(1,128)} %bitcast.2, s32[1,128]{1,0:T(1,128)} %bitcast.3, s32[160]{0:T(256)} %order_hbm.1), custom_call_target="tpu_custom_call" | custom-call | tf_op jit(solution)/shard_map/pallas_call | solution.py:387
  84.0 1.5 %copy.7 = f32[10,2,8,128]{3,2,1,0:T(8,128)} copy(f32[10,2,8,128]{3,2,1,0:T(8,128)} %shard_map.55) | data formatting | bytes 163840

commit v3 on v2

--- a/solution.py
+++ b/solution.py
@@ -8,6 +8,7 @@
 MESH = pl.DeviceIdType.MESH
 time_step = 0.1
 O = 128
+LEVELS = 32766.0
 B = 10
 ROWS = B * O
 CHUNKS = ((0, 6), (6, 4))
@@ -37,8 +38,8 @@
     g_hbm, ham_hbm, inter_hbm, partner_hbm, order_hbm, out,
     g, ham, inter, partner, order,
     send_a, core_a, comb_a, z_a, piece_a, f_prev, w, wh, part,
-    core_b, comb_b, z_b, sum_b, piece_b, f_new, z_d, sum_d,
-    load_sem, small_sem, core_ss, core_rs, a_ss, a_rs, z_ss, z_rs, t_ss, t_rs, all_ss, all_rs, *chunked,
+    core_b, comb_b, code_b, z_b, scale, scales, shift_b, piece_b, f_new, code_d, z_d,
+    load_sem, small_sem, core_ss, core_rs, a_ss, a_rs, s_ss, s_rs, z_ss, z_rs, t_ss, t_rs, all_ss, all_rs, *chunked,
 ):
     bf16 = jnp.bfloat16
     f32 = jnp.float32
@@ -69,8 +70,6 @@
     around = [((x + dx) % 4 * 4 + (y + dy) % 4, c) for dx, dy in AROUND]
 
     barrier = pltpu.get_barrier_semaphore()
-    up = (r, 2 * ((z + 1) % 8) + k)
-    down = (r, 2 * ((z + 7) % 8) + k)
     peers = [to, source] + [(r, 2 * ((z + d) % 8) + k) for d in FAR] + around + [other]
     for peer in peers:
         pl.semaphore_signal(barrier, inc=1, device_id=peer, device_id_type=MESH)
@@ -114,35 +113,42 @@
     def to_other(src, dst, phase, ch):
         return remote(src, dst, core_ss.at[phase, ch], core_rs.at[phase, ch], other)
 
-    def chain(comb, own, slots, sums, box, halve, phase, ch, step):
-        for way, (sign, device) in enumerate(((1, up), (7, down))):
-            whole = own((z + sign * (4 - step)) % 8)
-            if step == 0:
-                src = comb.at[halve(whole, way)]
-                dst = slots.at[(way, 0) + halve(box, way)]
-            else:
-                links[phase, ch, way, step - 1].wait_recv()
-                sums[(way, step - 1) + box] = comb[whole]
-                came = halve(box, way) if step == 1 else box
-                there = (way, step - 1) + came
-                sums[there] = sums[there] + slots[there]
-                src = sums.at[(way, step - 1) + box]
-                dst = slots.at[(way, step) + box]
-            links[phase, ch, way, step] = remote(
-                src, dst, z_ss.at[phase, ch, way, step], z_rs.at[phase, ch, way, step], device
-            )
-
-    def chained(comb, own, slots, box, phase, ch):
-        total = comb[own(z)]
-        for way in range(2):
-            links[phase, ch, way, 3].wait_recv()
-            total = total + slots[(way, 3) + box]
+    def code(piece_of, rows_at, coded, scale, phase, ch):
+        for zz in range(8):
+            term = piece_of(zz)
+            most = jnp.max(jnp.max(jnp.abs(term), axis=0, keepdims=True), axis=1, keepdims=True)
+            most = jnp.maximum(most, 1e-30)
+            term = term * (LEVELS / most)
+            coded[zz, rows_at] = (term + jnp.where(term >= 0, 0.5, -0.5)).astype(jnp.int32).astype(jnp.int16)
+            scale[phase, ch, zz] = jnp.broadcast_to(most * (1 / LEVELS), (8, O))
+
+    def over_z(coded, rows_at, slots, phase, ch):
+        copies = []
+        for d in FAR:
+            zz = (z + d) % 8
+            device = (r, 2 * zz + k)
+            copies.append((
+                d,
+                remote(
+                    scale.at[phase, ch, zz], scales.at[phase, ch, d - 1],
+                    s_ss.at[phase, ch, d - 1], s_rs.at[phase, ch, d - 1], device,
+                ),
+                remote(
+                    coded.at[zz, rows_at], slots.at[d - 1, rows_at],
+                    z_ss.at[phase, ch, d - 1], z_rs.at[phase, ch, d - 1], device,
+                ),
+            ))
+        return copies
+
+    def summed(total, copies, rows_at, slots, phase, ch):
+        for d, first_copy, second_copy in copies:
+            first_copy.wait_recv()
+            second_copy.wait_recv()
+            unit = scales[phase, ch, d - 1, :1]
+            if total.shape[1] > O:
+                unit = jnp.concatenate([unit, unit], axis=1)
+            total = total + slots[d - 1, rows_at].astype(jnp.int32).astype(f32) * unit
         return total
-
-    links = {}
-
-    def lane_half(index, way):
-        return index + (pl.ds(way * O, O),)
 
     def turn(src, f, phase, ch):
         return remote(src, f.at[piece(ch, q_out)], t_ss.at[phase, ch], t_rs.at[phase, ch], to)
@@ -233,7 +239,7 @@
         acc += jnp.dot(left, wh[0], preferred_element_type=f32)
         return acc
 
-    def flow(finish, f, phase):
+    def flow(finish, f, phase, after):
         turns = []
         spreads = []
         for ch in range(NC):
@@ -244,6 +250,8 @@
                 spreads.append(spread(f, phase, ch - 1))
         turns[NC - 1].wait_recv()
         spreads.append(spread(f, phase, NC - 1))
+        for ch in range(NC):
+            after(ch)
         return spreads
 
     def finish_a(ch):
@@ -253,7 +261,11 @@
             total = total + z_a[d - 1, near(ch)]
         piece_a[near(ch)] = total
 
-    a_all = flow(finish_a, f_prev, 0)
+    def after_a(ch):
+        base = piece_a[near(ch)]
+        shift_b[near(ch)] = hamiltonian(base)
+
+    a_all = flow(finish_a, f_prev, 0, after_a)
 
     def self_energy(f, ch):
         first, count = CHUNKS[ch]
@@ -294,11 +306,7 @@
             contract(0, B, ch, ch == 0)
     b_core = []
 
-    def chain_b(ch, step):
-        chain(
-            comb_b, lambda zz: (core_piece(ch, zz),), z_b, sum_b, (near(ch),), lane_half, 1, ch, step
-        )
-
+    b_z = []
     for ch in range(NC):
         first, n = CHUNKS[ch]
         contract(first + (1 - k) * (n // 2), n // 2, NC - 1, False)
@@ -306,25 +314,27 @@
         contract(first + k * (n // 2), n // 2, NC - 1, False)
         b_core[ch].wait_recv()
         comb_b[core_near(ch)] = part[half(ch, k)] + core_b[core_near(ch)]
-        chain_b(ch, 0)
-    for step in range(1, 4):
-        for ch in range(NC):
-            chain_b(ch, step)
+        code(
+            lambda zz: comb_b[first * 64 + zz * n * 8:first * 64 + (zz + 1) * n * 8],
+            near(ch), code_b, scale, 0, ch,
+        )
+        b_z.append(over_z(code_b, near(ch), z_b, 0, ch))
     for copy in b_core:
         copy.wait_send()
     sent[:] = [copy for copy in sent if not any(copy is done for done in b_core)]
 
     def finish_b(ch):
         first, n = CHUNKS[ch]
-        base = piece_a[near(ch)]
-        shift = hamiltonian(base)
-        total = chained(comb_b, lambda zz: (core_piece(ch, zz),), z_b, (near(ch),), 1, ch)
-        base = base.astype(f32)
-        new = (base + time_step * (shift + total)).astype(bf16)
-        piece_b[near(ch)] = new
-        part[piece(ch, q_out)] += (2 / time_step) * base + shift + hamiltonian(new)
-
-    b_all = flow(finish_b, f_new, 1)
+        total = summed(comb_b[core_piece(ch, z)], b_z[ch], near(ch), z_b, 0, ch)
+        base = piece_a[near(ch)].astype(f32)
+        piece_b[near(ch)] = (base + time_step * (shift_b[near(ch)] + total)).astype(bf16)
+
+    def after_b(ch):
+        base = piece_a[near(ch)].astype(f32)
+        rest = (2 / time_step) * base + shift_b[near(ch)] + hamiltonian(piece_b[near(ch)])
+        part[piece(ch, q_out)] += rest
+
+    b_all = flow(finish_b, f_new, 1, after_b)
 
     for ch in range(NC):
         received(b_all[ch])
@@ -333,26 +343,15 @@
             contract(0, B, ch, False)
     d_core = []
 
-    def box_d(ch):
-        first, n = CHUNKS[ch]
-        return (pl.ds(first * 16, n * 16),)
-
-    def chain_d(ch, step):
-        first, n = CHUNKS[ch]
-
-        def row_half(index, way):
-            start = first * 16 if len(index) == 1 else 0
-            return index[:-1] + (pl.ds(start + way * n * 8, n * 8),)
-
-        chain(
-            comb_d[ch], lambda zz: (zz, pl.ds(0, n * 16)), z_d, sum_d, box_d(ch), row_half, 2, ch, step
-        )
+    d_z = []
 
     def over_z_d(ch):
         first, n = CHUNKS[ch]
         d_core[ch].wait_recv()
         comb_d[ch][...] = send_d[ch][k] + core_d[ch][...]
-        chain_d(ch, 0)
+        at = pl.ds(first * 16, n * 16)
+        code(lambda zz: comb_d[ch][zz], at, code_d, scale, 1, ch)
+        d_z.append(over_z(code_d, at, z_d, 1, ch))
 
     for ch in range(NC):
         first, n = CHUNKS[ch]
@@ -367,12 +366,9 @@
         if ch > 0:
             over_z_d(ch - 1)
     over_z_d(NC - 1)
-    for step in range(1, 4):
-        for ch in range(NC):
-            chain_d(ch, step)
-    for ch in range(NC):
-        first, n = CHUNKS[ch]
-        total = chained(comb_d[ch], lambda zz: (zz, pl.ds(0, n * 16)), z_d, box_d(ch), 2, ch)
+    for ch in range(NC):
+        first, n = CHUNKS[ch]
+        total = summed(comb_d[ch][z], d_z[ch], pl.ds(first * 16, n * 16), z_d, 1, ch)
         out[first:first + n] = (0.5 * time_step) * total.reshape(n, 2, 8, O)
 
     for copy in sent:
@@ -406,20 +402,25 @@
             vmem((ROWS, 2 * O), f32),
             vmem((ROWS // 2, 2 * O), f32),
             vmem((ROWS // 2, 2 * O), f32),
-            vmem((2, 4, ROWS // 16, 2 * O), f32),
-            vmem((2, 3, ROWS // 16, 2 * O), f32),
+            vmem((8, ROWS // 16, 2 * O), jnp.int16),
+            vmem((7, ROWS // 16, 2 * O), jnp.int16),
+            vmem((2, NC, 8, 8, O), f32),
+            vmem((2, NC, 7, 8, O), f32),
+            vmem((ROWS // 16, 2 * O), f32),
             vmem((ROWS // 16, 2 * O), bf16),
             vmem((ROWS, 2 * O), bf16),
-            vmem((2, 4, 16 * B, O), f32),
-            vmem((2, 3, 16 * B, O), f32),
+            vmem((8, 16 * B, O), jnp.int16),
+            vmem((7, 16 * B, O), jnp.int16),
             dma((B,)),
             dma((4,)),
             dma((3, NC)),
             dma((3, NC)),
             dma((NC, 7)),
             dma((NC, 7)),
-            dma((3, NC, 2, 4)),
-            dma((3, NC, 2, 4)),
+            dma((2, NC, 7)),
+            dma((2, NC, 7)),
+            dma((2, NC, 7)),
+            dma((2, NC, 7)),
             dma((2, NC)),
             dma((2, NC)),
             dma((2, NC, 15)),

time: 85.6 us -> 80.5 us (0.940)
  Pallas kernels: 84 us -> 78.9 us
    pallas_call x1, Pallas kernels: 84 us -> 78.9 us  [shards(): pl.pallas_call(kernel, out_shape=jax.ShapeDtypeStruct((B, 2, 8, O), f32),...]
where the time goes in v3:
time: 80.5 us; the launch traced here: 80.4 us
  Pallas kernels  78.9 us (98%)
  local copies, waits for them, and re-layouts  1.53 us (2%)
    pallas_call x1, Pallas kernels, shards(): pl.pallas_call(kernel, out_shape=jax.ShapeDtypeStruct((B, 2, 8, O), f32),...  78.9 us

profile of v3, /device:TPU:1, one launch (start us, length us, event | category | flops | bytes accessed | tf_op | source)
XLA Modules:
  0.0 80.4 jit_solution(10021090298228915737)
XLA Ops:
  0.0 78.9 %shard_map.55 = f32[10,2,8,128]{3,2,1,0:T(8,128)} custom-call(bf16[10,10,2,128,128]{4,3,2,1,0:T(8,128)(2,1)} %g_hbm.1, f32[2,128,128]{2,1,0:T(8,128)} %ham_hbm.1, f32[1,128]{1,0:T(1,128)} %bitcast.2, s32[1,128]{1,0:T(1,128)} %bitcast.3, s32[160]{0:T(256)} %order_hbm.1), custom_call_target="tpu_custom_call" | custom-call | tf_op jit(solution)/shard_map/pallas_call | solution.py:383
  78.9 1.5 %copy.7 = f32[10,2,8,128]{3,2,1,0:T(8,128)} copy(f32[10,2,8,128]{3,2,1,0:T(8,128)} %shard_map.55) | data formatting | bytes 163840

commit v4 on v3

--- a/solution.py
+++ b/solution.py
@@ -11,7 +11,7 @@
 LEVELS = 32766.0
 B = 10
 ROWS = B * O
-CHUNKS = ((0, 6), (6, 4))
+CHUNKS = ((0, 4), (4, 6))
 NC = len(CHUNKS)
 FAR = (4, 3, 5, 2, 6, 1, 7)
 AROUND = sorted(
@@ -311,6 +311,8 @@
         first, n = CHUNKS[ch]
         contract(first + (1 - k) * (n // 2), n // 2, NC - 1, False)
         b_core.append(to_other(part.at[half(ch, 1 - k)], core_b.at[core_near(ch)], 1, ch))
+    for ch in range(NC):
+        first, n = CHUNKS[ch]
         contract(first + k * (n // 2), n // 2, NC - 1, False)
         b_core[ch].wait_recv()
         comb_b[core_near(ch)] = part[half(ch, k)] + core_b[core_near(ch)]
@@ -355,6 +357,8 @@
 
     for ch in range(NC):
         first, n = CHUNKS[ch]
+        if ch > 0:
+            over_z_d(ch - 1)
         contract(first, n, NC - 1, False)
         for j in range(first, first + n):
             for o in range(2):
@@ -363,8 +367,6 @@
                 for kk in range(2):
                     send_d[ch][kk, :, at] = turned[:, kk]
         d_core.append(to_other(send_d[ch].at[1 - k], core_d[ch], 2, ch))
-        if ch > 0:
-            over_z_d(ch - 1)
     over_z_d(NC - 1)
     for ch in range(NC):
         first, n = CHUNKS[ch]

time: 80.5 us -> 78.5 us (0.975)
  Pallas kernels: 78.9 us -> 76.8 us
    pallas_call x1, Pallas kernels: 78.9 us -> 76.8 us  [shards(): pl.pallas_call(kernel, out_shape=jax.ShapeDtypeStruct((B, 2, 8, O), f32),...]
where the time goes in v4:
time: 78.5 us; the launch traced here: 78.4 us
  Pallas kernels  76.8 us (98%)
  local copies, waits for them, and re-layouts  1.53 us (2%)
    pallas_call x1, Pallas kernels, shards(): pl.pallas_call(kernel, out_shape=jax.ShapeDtypeStruct((B, 2, 8, O), f32),...  76.8 us

profile of v4, /device:TPU:1, one launch (start us, length us, event | category | flops | bytes accessed | tf_op | source)
XLA Modules:
  0.0 78.4 jit_solution(3080763776637645089)
XLA Ops:
  0.0 76.8 %shard_map.55 = f32[10,2,8,128]{3,2,1,0:T(8,128)} custom-call(bf16[10,10,2,128,128]{4,3,2,1,0:T(8,128)(2,1)} %g_hbm.1, f32[2,128,128]{2,1,0:T(8,128)} %ham_hbm.1, f32[1,128]{1,0:T(1,128)} %bitcast.2, s32[1,128]{1,0:T(1,128)} %bitcast.3, s32[160]{0:T(256)} %order_hbm.1), custom_call_target="tpu_custom_call" | custom-call | tf_op jit(solution)/shard_map/pallas_call | solution.py:385
  76.8 1.5 %copy.7 = f32[10,2,8,128]{3,2,1,0:T(8,128)} copy(f32[10,2,8,128]{3,2,1,0:T(8,128)} %shard_map.55) | data formatting | bytes 163840

commit v5 on v4

--- a/solution.py
+++ b/solution.py
@@ -57,9 +57,6 @@
         pltpu.make_async_copy(a, b, small_sem.at[i + 1])
         for i, (a, b) in enumerate(((ham_hbm, ham), (inter_hbm, inter), (partner_hbm, partner)))
     ]
-    for load in loads:
-        load.start()
-
     n_out = 2 * ((r // 2 - z + 8) % 8) + k
     to = ((x + look_up(STEP_X, n_out)) % 4 * 4 + (y + look_up(STEP_Y, n_out)) % 4, r)
     q_out = k * 8 + z
@@ -73,6 +70,8 @@
     peers = [to, source] + [(r, 2 * ((z + d) % 8) + k) for d in FAR] + around + [other]
     for peer in peers:
         pl.semaphore_signal(barrier, inc=1, device_id=peer, device_id_type=MESH)
+    for load in loads:
+        load.start()
 
     def rows(start, size):
         return pl.ds(pl.multiple_of(start, 16), size)

time: 78.5 us -> 78.8 us (level)
  no operation moved by 1% of the time
where the time goes in v5:
time: 78.8 us; the launch traced here: 78.6 us
  Pallas kernels  77.1 us (98%)
  local copies, waits for them, and re-layouts  1.53 us (2%)
    pallas_call x1, Pallas kernels, shards(): pl.pallas_call(kernel, out_shape=jax.ShapeDtypeStruct((B, 2, 8, O), f32),...  77.1 us

profile of v5, /device:TPU:1, one launch (start us, length us, event | category | flops | bytes accessed | tf_op | source)
XLA Modules:
  0.0 78.6 jit_solution(14884082386614610481)
XLA Ops:
  0.0 77.1 %shard_map.55 = f32[10,2,8,128]{3,2,1,0:T(8,128)} custom-call(bf16[10,10,2,128,128]{4,3,2,1,0:T(8,128)(2,1)} %g_hbm.1, f32[2,128,128]{2,1,0:T(8,128)} %ham_hbm.1, f32[1,128]{1,0:T(1,128)} %bitcast.2, s32[1,128]{1,0:T(1,128)} %bitcast.3, s32[160]{0:T(256)} %order_hbm.1), custom_call_target="tpu_custom_call" | custom-call | tf_op jit(solution)/shard_map/pallas_call | solution.py:384
  77.1 1.5 %copy.7 = f32[10,2,8,128]{3,2,1,0:T(8,128)} copy(f32[10,2,8,128]{3,2,1,0:T(8,128)} %shard_map.55) | data formatting | bytes 163840
